TPU v7x, 256 devices: a whole 4x4x8 slice. The times are simulated.
256 devices in a mesh: wave: 32 (over z, y), lev: 8 (over x, core).
Axes of the slice: x: 4, y: 4, z: 8, core: 2. Of those that a mesh axis runs over, the one named last changes fastest.
Arguments:
- grid_field: bfloat16 [32, 2, 1024, 4224], P('lev', None, 'wave'), may hold values from -6 to 6
- legendre: bfloat16 [512, 1025, 1024], P(('wave', 'lev')), may hold values from -0.1875 to 0.1875
- wave_groups: int32 [512], P(('wave', 'lev')), may hold values from 0 to 511, each once
- lat_weights: float32 [1024], replicated, may hold values from 0.5 to 2
- cycle_points: int32 [2, 1024], replicated, may hold values from 16 to 4116, as said below
- diffusion: float32 [32], replicated, may hold values from 0.5 to 8
Outputs:
- spectrum: float32 [512, 32, 2, 1025], P(('wave', 'lev'))
- grid_out: bfloat16 [32, 2, 1024, 4224], P('lev', None, 'wave')
Inputs may be any that keep to these rules, and one draw needn't show every extreme that they name: `wave_groups`: a permutation. cycle_points[h, j] = 16 + 4 j + 4 r with r one of 0, 1, 2; r is 0 on the polar cycles and 2 on the cycles beside the equator.
All inputs are finite; a program needn't handle non-finite values.
Results may differ from a plain program's by a relative error of at most 0.0075.
Values may be sent and summed in bfloat16 or wider, within the bound.
A program may use at most 128 MiB of HBM per device.

v0:
```python
import math

import jax
import jax.numpy as jnp
import ml_dtypes
import numpy as np
from jax import lax
from jax.experimental import pallas as pl
from jax.experimental.pallas import tpu as pltpu
from jax.sharding import PartitionSpec as P

WAVES = 1024
PAIRS = 512
NLON = 4224
HALF = NLON // 2
WIDE = 2176
ROWS = 1025
ROWP = 1152
NWAVE = 32
NLEV = 8
MESH = pl.DeviceIdType.MESH
F32 = jnp.float32
BF16 = jnp.bfloat16
NT = (((1,), (1,)), ((), ()))
NN = (((1,), (0,)), ((), ()))


def basis_tables():
    pairs = np.arange(PAIRS, dtype=np.int64)
    points = np.arange(HALF, dtype=np.int64)
    tables = np.zeros((2, 2, PAIRS, WIDE), np.float32)
    for p, waves in enumerate((2 * pairs, WAVES - 1 - 2 * pairs)):
        angles = (waves[:, None] * points[None, :] % NLON) * (2.0 * math.pi / NLON)
        tables[p, 0, :, :HALF] = np.cos(angles) / math.sqrt(NLON)
        tables[p, 1, :, :HALF] = -np.sin(angles) / math.sqrt(NLON)
    return tables.reshape(2, 2 * PAIRS, WIDE).astype(ml_dtypes.bfloat16)


def select8(index, values):
    result = jnp.int32(values[0])
    for k in range(1, len(values)):
        result = jnp.where(index == k, values[k], result)
    return result


Z_ORDER = (0, 1, 7, 2, 6, 3, 5, 4)
Y_ORDER = (0, 1, 3, 2)


def lev_offset(index):
    return select8(index % 4, Y_ORDER), index // 4


def lev_at(l, index):
    dx, dc = lev_offset(index)
    return (l // 2 + dx) % 4 * 2 + (l % 2 + dc) % 2


def lev_from(l, index):
    dx, dc = lev_offset(index)
    return (l // 2 + 4 - dx) % 4 * 2 + (l % 2 + dc) % 2


def wave_at(w, index):
    dz = select8(index % 8, Z_ORDER)
    dy = select8(index // 8, Y_ORDER)
    return (w // 4 + dz) % 8 * 4 + (w % 4 + dy) % 4


def sub_iota(shape):
    return lax.broadcasted_iota(jnp.int32, shape, len(shape) - 2)


def lane_iota(shape):
    return lax.broadcasted_iota(jnp.int32, shape, len(shape) - 1)


def swap_lane(a0, a1, a2, a3):
    lane = lane_iota(a0.shape)
    low64 = lane < 64
    low32 = lane % 64 < 32

    def roll(x, s):
        return pltpu.roll(x, s, 1)

    lo0 = jnp.where(low64, a0, roll(a2, 64))
    lo1 = jnp.where(low64, a1, roll(a3, 64))
    hi0 = jnp.where(low64, roll(a0, 64), a2)
    hi1 = jnp.where(low64, roll(a1, 64), a3)
    return (
        jnp.where(low32, lo0, roll(lo1, 32)),
        jnp.where(low32, roll(lo0, 96), lo1),
        jnp.where(low32, hi0, roll(hi1, 32)),
        jnp.where(low32, roll(hi0, 96), hi1),
    )


def exchange(
    field_hbm, leg_hbm, table_hbm, ids, weights, points, diffusion,
    spec_hbm, back,
    field, raw, leg, last, table, fold, pairs, send_f, recv_f, oper, damp, dope, spec, send_b,
    recv_b, rows, turned, onehot, column, gat1, gat2, gatv, gats,
    s_table, s_field, s_leg, s_local, s_spec, s_g1s, s_g1r, s_g2s, s_g2r, s_fs, s_fr, s_bs, s_br,
):
    w = lax.axis_index("wave")
    l = lax.axis_index("lev")
    me = w * NLEV + l

    field_copy = pltpu.make_async_copy(field_hbm, field, s_field)
    field_copy.start()
    table_copies = [
        pltpu.make_async_copy(table_hbm.at[p], table.at[p], s_table.at[p]) for p in range(2)
    ]
    table_copies[0].start()
    leg_copy = pltpu.make_async_copy(leg_hbm, raw, s_leg)

    barrier = pltpu.get_barrier_semaphore()

    def greet_lev(i, c):
        pl.semaphore_signal(barrier, inc=1, device_id=(w, (l + i) % NLEV), device_id_type=MESH)
        return c

    def greet_wave(i, c):
        pl.semaphore_signal(barrier, inc=1, device_id=((w + i) % NWAVE, l), device_id_type=MESH)
        return c

    lax.fori_loop(1, NLEV, greet_lev, 0)
    lax.fori_loop(1, NWAVE, greet_wave, 0)

    a0 = ids[0]
    a1 = ids[1]
    t0 = jnp.where(a0 % 2 == 0, a0 // 2, (WAVES - 1 - a0) // 2)
    t1 = jnp.where(a1 % 2 == 0, a1 // 2, (WAVES - 1 - a1) // 2)
    flat = sub_iota((8, 128)) * 128 + lane_iota((8, 128))
    tile = jnp.where(flat == 2 * me, t0, 0) + jnp.where(flat == 2 * me + 1, t1, 0)
    tile = tile + jnp.where(flat == PAIRS + t0, 2 * me, 0)
    tile = tile + jnp.where(flat == PAIRS + t1, 2 * me + 1, 0)
    gat1[l] = tile

    band = pl.multiple_of(w // 4 * 128, 128)
    turn = (4 - w % 4) % 4 * 32
    lane1 = lane_iota((8, 128))

    def spread(row):
        moved = pltpu.roll(jnp.broadcast_to(row, (8, 128)), turn, 1)
        first = jnp.where(lane1 < 32, moved, jnp.zeros_like(moved))
        twice = first + pltpu.roll(first, 32, 1)
        return twice + pltpu.roll(twice, 64, 1)

    band_weights = spread(weights[:, pl.ds(band, 128)])
    band_points = [spread(points[h:h + 1, pl.ds(band, 128)]) for h in range(2)]

    pl.semaphore_wait(barrier, NLEV - 1 + NWAVE - 1)

    def send_g1(i, c):
        pltpu.make_async_remote_copy(
            src_ref=gat1.at[l], dst_ref=gat1.at[l], send_sem=s_g1s, recv_sem=s_g1r,
            device_id=(w, (l + i) % NLEV), device_id_type=MESH,
        ).start()
        return c

    lax.fori_loop(1, NLEV, send_g1, 0)

    field_copy.wait()
    table_copies[1].start()

    def fold_body(i, c):
        f = i // 4
        h = i // 2 % 2
        j = pl.multiple_of(i % 2 * 16, 16)
        first = field[f, h, pl.ds(j, 16), 0:WIDE].astype(F32)
        second = field[f, h, pl.ds(j, 16), NLON - WIDE:NLON].astype(F32)
        second = pltpu.roll(second, HALF, 1)
        row = pl.multiple_of(h * 128 + f * 32 + j, 16)
        fold[0, pl.ds(row, 16), :] = (first + second).astype(BF16)
        fold[1, pl.ds(row, 16), :] = (first - second).astype(BF16)
        return c

    lax.fori_loop(0, 16, fold_body, 0)

    g1 = pltpu.make_async_remote_copy(
        src_ref=gat1.at[pl.ds(0, NLEV - 1)], dst_ref=gat1.at[pl.ds(0, NLEV - 1)], send_sem=s_g1s,
        recv_sem=s_g1r, device_id=(w, l), device_id_type=MESH,
    )
    g1.wait_send()
    g1.wait_recv()
    total = gat1[0]
    for i in range(1, NLEV):
        total = total + gat1[i]
    gat2[w] = total

    def send_g2(i, c):
        pltpu.make_async_remote_copy(
            src_ref=gat2.at[w], dst_ref=gat2.at[w], send_sem=s_g2s, recv_sem=s_g2r,
            device_id=((w + i) % NWAVE, l), device_id_type=MESH,
        ).start()
        return c

    lax.fori_loop(1, NWAVE, send_g2, 0)

    def twice_wave(p, pair):
        return 4 * pair if p == 0 else 2 * (WAVES - 1) - 4 * pair

    def transform(p):
        for part in range(2):
            def body(m, c, part=part):
                first = pl.multiple_of(m * 256, 256)
                start = pl.multiple_of(part * PAIRS + m * 256, 256)
                out = lax.dot_general(
                    table[p, pl.ds(start, 256), :], fold[p], NT, preferred_element_type=F32
                )
                twice = twice_wave(p, first + sub_iota((256, 128)))
                north = jnp.where(twice < band_points[0][0:1, :], out[:, :128], 0.0)
                south = jnp.where(twice < band_points[1][0:1, :], out[:, 128:], 0.0)
                scale = band_weights[0:1, :]
                pairs[pl.ds(first, 256), 2 * p + part, :] = (north + south) * scale
                pairs[pl.ds(first, 256), 4 + 2 * p + part, :] = (north - south) * scale
                return c

            lax.fori_loop(0, 2, body, 0)

    table_copies[0].wait()
    transform(0)
    table_copies[1].wait()
    leg_copy.start()
    transform(1)

    g2 = pltpu.make_async_remote_copy(
        src_ref=gat2.at[pl.ds(0, NWAVE - 1)], dst_ref=gat2.at[pl.ds(0, NWAVE - 1)], send_sem=s_g2s,
        recv_sem=s_g2r, device_id=(w, l), device_id_type=MESH,
    )
    g2.wait_send()
    g2.wait_recv()
    total = gat2[0]
    for i in range(1, NWAVE):
        total = total + gat2[i]
    gatv[...] = jnp.clip(total, 0, PAIRS - 1)
    ids_copy = pltpu.make_async_copy(gatv, gats, s_local)
    ids_copy.start()
    ids_copy.wait()

    def packed(d):
        first = gats[d // 64, 2 * d % 128]
        second = gats[d // 64, 2 * d % 128 + 1]
        return jnp.concatenate([pairs[first], pairs[second]], axis=0).astype(BF16)

    recv_f[me] = packed(me)

    def send_forward(i, c):
        j = 256 - i
        w2 = wave_at(w, j % NWAVE)
        l2 = lev_at(l, j // NWAVE)
        d = w2 * NLEV + l2
        send_f[d] = packed(d)
        pltpu.make_async_remote_copy(
            src_ref=send_f.at[d], dst_ref=recv_f.at[me], send_sem=s_fs, recv_sem=s_fr.at[l],
            device_id=(w2, l2), device_id_type=MESH,
        ).start()
        return c

    lax.fori_loop(1, 256, send_forward, 0)

    leg_copy.wait()

    def relay(i, c):
        k = pl.multiple_of(i * 16, 16)
        for ch in range(8):
            x = raw[pl.ds(k, 16), ch].astype(F32)
            for s in range(2):
                leg[s, pl.ds(k, 16), ch * 128:(ch + 1) * 128] = x[:, s, :].astype(BF16)
        return c

    lax.fori_loop(0, 64, relay, 0)
    for ch in range(8):
        x = raw[1024, ch].astype(F32)
        for s in range(2):
            last[s, :, ch * 128:(ch + 1) * 128] = jnp.broadcast_to(x[s:s + 1], (16, 128)).astype(BF16)

    def chosen(a, base, width):
        sub = sub_iota((8, width))
        k = base + lane_iota((8, width))
        is_a = k < WAVES - a
        parity = jnp.where(is_a, k % 2, (k + a) % 2)
        member = jnp.where(is_a, a % 2, 1 - a % 2)
        sel = (sub // 4 == parity) & (sub // 2 % 2 == member) & (k < ROWS)
        degree = jnp.where(is_a, a + k, k - 1)
        return sel, degree

    for s, a in enumerate((a0, a1)):
        sel, degree = chosen(a, 0, ROWP)
        level = degree.astype(F32)
        scaled = level * (level + 1.0) / (WAVES * (WAVES - 1.0))
        squared = scaled * scaled
        one = jnp.where(sel, 1.0, 0.0)

        def damp_body(f, c, s=s, squared=squared, one=one):
            row = pl.multiple_of(f * 8, 8)
            damp[s, pl.ds(row, 8), :] = one / (1.0 + diffusion[f] * squared)
            return c

        lax.fori_loop(0, 32, damp_body, 0)

    for b in range(4):
        holder = gatv[4 + b:5 + b, :]

        def onehot_body(i, c, b=b, holder=holder):
            start = pl.multiple_of(i * 128, 128)
            hit = start + sub_iota((128, 128)) == holder
            onehot[pl.ds(start, 128), b * 128:(b + 1) * 128] = jnp.where(hit, 1.0, 0.0).astype(BF16)
            return c

        lax.fori_loop(0, 4, onehot_body, 0)
    for h in range(2):
        column[h] = jnp.broadcast_to(band_points[h][0:1, :].astype(F32), (128, 128)).T

    def arrive(i, c):
        src = lev_from(l, 7 - i)

        def landed(count):
            pltpu.make_async_remote_copy(
                src_ref=send_f.at[pl.ds(0, count)], dst_ref=recv_f.at[pl.ds(0, count)],
                send_sem=s_fs, recv_sem=s_fr.at[src], device_id=(w, l), device_id_type=MESH,
            ).wait_recv()

        @pl.when(src == l)
        def _():
            landed(NWAVE - 1)

        @pl.when(src != l)
        def _():
            landed(NWAVE)

        for block in range(8):
            tiles = [recv_f[(4 * block + i) * NLEV + src].astype(F32) for i in range(4)]
            by_field = swap_lane(*tiles)
            for s in range(2):
                for pair in range(2):
                    row = pl.multiple_of(src * 32 + pair * 16, 16)
                    oper[s, pl.ds(row, 16), block * 128:(block + 1) * 128] = jnp.concatenate(
                        [
                            by_field[2 * pair][8 * s:8 * s + 8],
                            by_field[2 * pair + 1][8 * s:8 * s + 8],
                        ],
                        axis=0,
                    ).astype(BF16)
        return c

    lax.fori_loop(0, 8, arrive, 0)

    def pick(s, a, x, start, width):
        sel, _ = chosen(a, start, width)
        lanes = pl.ds(start, width)
        for i in range(16):
            damped = []
            for f in (2 * i, 2 * i + 1):
                y = jnp.where(sel, x[8 * f:8 * f + 8], 0.0)
                y = y + pltpu.roll(y, 4, 0)
                y = y + pltpu.roll(y, 2, 0)
                if width == 128:
                    spec[s, f, :, 1024:ROWS] = y[0:2, 0:1]
                else:
                    spec[s, f, :, lanes] = y[0:2]
                damped.append(y * damp[s, 8 * f:8 * f + 8, lanes])
            dope[s, 16 * i:16 * i + 16, lanes] = jnp.concatenate(damped, axis=0).astype(BF16)

    def product(n, c):
        start = pl.multiple_of(n * 256, 256)
        for s, a in enumerate((a0, a1)):
            x = lax.dot_general(
                oper[s], leg[s, pl.ds(start, 256), :], NT, preferred_element_type=F32
            )
            pick(s, a, x, start, 256)
        return c

    lax.fori_loop(0, 4, product, 0)
    for s, a in enumerate((a0, a1)):
        rhs = jnp.concatenate([last[s]] * 8, axis=0)
        x = lax.dot_general(oper[s], rhs, NT, preferred_element_type=F32)
        pick(s, a, x, 1024, 128)
    spec_copy = pltpu.make_async_copy(spec, spec_hbm, s_spec)
    spec_copy.start()

    def inverse(i, c):
        n = (w // 8 + select8(i, (2, 1, 3, 0))) % 4
        start = pl.multiple_of(n * 256, 256)
        sign = jnp.where(sub_iota((1, 8, 256)) < 4, 1.0, -1.0)
        hemis = []
        for s in range(2):
            x = lax.dot_general(
                dope[s, :, 0:1024], leg[s, 0:1024, pl.ds(start, 256)], NN,
                preferred_element_type=F32,
            )
            edge = dope[s, :, 1024:ROWP].astype(F32)[:, 0:1]
            x = x + edge * last[s, :, pl.ds(start, 256)].astype(F32)[0:1]
            x = x.reshape(32, 8, 256)
            hemis.append(x * sign + pltpu.roll(x, 4, 1))
        for l2 in range(8):
            for half in range(2):
                tiles = []
                for f in range(4):
                    tiles.append(
                        jnp.concatenate(
                            [
                                hemis[s][4 * l2 + f, :, half * 128:(half + 1) * 128]
                                for s in range(2)
                            ],
                            axis=0,
                        )
                    )
                for u, x in enumerate(swap_lane(*tiles)):
                    send_b[(8 * n + 4 * half + u) * NLEV + l2] = x.astype(BF16)

        def send_back(m, c):
            w2 = 8 * n + m % 8
            l2 = lev_at(l, 7 - m // 8)
            d = w2 * NLEV + l2

            @pl.when(d != me)
            def _():
                pltpu.make_async_remote_copy(
                    src_ref=send_b.at[d], dst_ref=recv_b.at[me], send_sem=s_bs,
                    recv_sem=s_br.at[w // 8], device_id=(w2, l2), device_id_type=MESH,
                ).start()

            return c

        lax.fori_loop(0, 64, send_back, 0)
        return c

    lax.fori_loop(0, 4, inverse, 0)
    recv_b[me] = send_b[me]

    def returned(i, c):
        n = (w // 8 + 4 - select8(i, (2, 1, 3, 0))) % 4

        def landed(count):
            pltpu.make_async_remote_copy(
                src_ref=send_b.at[pl.ds(0, count)], dst_ref=recv_b.at[pl.ds(0, count)],
                send_sem=s_bs, recv_sem=s_br.at[n], device_id=(w, l), device_id_type=MESH,
            ).wait_recv()

        @pl.when(i == 3)
        def _():
            landed(63)

        @pl.when(i != 3)
        def _():
            landed(64)

        for d in range(64):
            both = recv_b[64 * n + d].astype(F32)
            rows[2 * d] = both[0:8]
            rows[2 * d + 1] = both[8:16]
        lanes = pl.multiple_of(n * 128, 128)
        for j in range(8):
            turned[j, :, pl.ds(lanes, 128)] = rows[:, j, :].T.astype(BF16)
        return c

    lax.fori_loop(0, 4, returned, 0)

    for h in range(2):
        for p in range(2):
            for r in range(2):
                x = lax.dot_general(
                    turned[4 * h + 2 * p + r], onehot[...], NN, preferred_element_type=F32
                )
                limit = jnp.concatenate([column[h]] * 4, axis=1)
                twice = twice_wave(p, lane_iota((128, PAIRS)))
                x = jnp.where(twice.astype(F32) < limit, x, 0.0)
                x = x * (jnp.where(twice == 0, 1.0, 2.0) if p == 0 else 2.0)
                back[p, h * 128:(h + 1) * 128, r * PAIRS:(r + 1) * PAIRS] = x.astype(BF16)

    spec_copy.wait()
    pltpu.make_async_remote_copy(
        src_ref=send_f.at[pl.ds(0, 255)], dst_ref=recv_f.at[pl.ds(0, 255)], send_sem=s_fs,
        recv_sem=s_g1r, device_id=(w, l), device_id_type=MESH,
    ).wait_send()
    pltpu.make_async_remote_copy(
        src_ref=send_b.at[pl.ds(0, 255)], dst_ref=recv_b.at[pl.ds(0, 255)], send_sem=s_bs,
        recv_sem=s_g1r, device_id=(w, l), device_id_type=MESH,
    ).wait_send()


BLOCKS = [(0, 2048, 128)] + [(1 + n, 256 * n, 256) for n in range(8)]


def synthesis(
    back, table_hbm, spec_in, grid_hbm, spec_out, table, outv, s_table, s_spec, s_out
):
    copies = []
    for i, start, width in BLOCKS:
        copies.append(
            pltpu.make_async_copy(
                table_hbm.at[:, :, pl.ds(start, width)], table.at[:, :, pl.ds(start, width)],
                s_table.at[i],
            )
        )
        copies[-1].start()
    spec_copy = pltpu.make_async_copy(spec_in, spec_out, s_spec)
    spec_copy.start()
    outs = []

    def write(x, start, width):
        for h in range(2):
            for f in range(4):
                row = h * 128 + f * 32
                outv[f, h, :, start:start + width] = x[row:row + 32].astype(BF16)
        outs.append(
            pltpu.make_async_copy(
                outv.at[:, :, :, pl.ds(start, width)], grid_hbm.at[:, :, :, pl.ds(start, width)],
                s_out.at[len(outs)],
            )
        )
        outs[-1].start()

    tail = None
    before = None
    for i, start, width in BLOCKS:
        copies[i].wait()
        x = jnp.dot(back[0], table[0, :, start:start + width], preferred_element_type=F32)
        y = jnp.dot(back[1], table[1, :, start:start + width], preferred_element_type=F32)
        total = x + y
        differ = pltpu.roll(x - y, 64, 1)
        if i == 0:
            tail = differ
            before = total
        else:
            low = lane_iota((256, 128)) < 64
            write(total, start, 256)
            edge = jnp.where(low, before, differ[:, :128])
            write(jnp.concatenate([edge, differ[:, 128:]], axis=1), 2048 + start, 256)
            before = differ[:, :128]
    write(jnp.where(lane_iota((256, 128)) < 64, before, tail), 4096, 128)
    for copy in outs:
        copy.wait()
    spec_copy.wait()


def shards(grid_field, legendre, wave_groups, lat_weights, cycle_points, diffusion):
    dma = pltpu.SemaphoreType.DMA
    vmem = pl.BlockSpec(memory_space=pltpu.VMEM)
    smem = pl.BlockSpec(memory_space=pltpu.SMEM)
    hbm = pl.BlockSpec(memory_space=pl.ANY)
    table = jnp.asarray(basis_tables())
    by_row = legendre.reshape(2, ROWS, 8, 128).transpose(1, 2, 0, 3)
    spectrum_shape = (2, 32, 2, ROWS)
    spectrum, back = pl.pallas_call(
        exchange,
        out_shape=(
            jax.ShapeDtypeStruct(spectrum_shape, F32),
            jax.ShapeDtypeStruct((2, 256, 1024), BF16),
        ),
        in_specs=[hbm, hbm, hbm, smem, vmem, vmem, smem],
        out_specs=(hbm, vmem),
        scratch_shapes=[
            pltpu.VMEM((4, 2, 32, NLON), BF16),
            pltpu.VMEM((ROWS, 8, 2, 128), BF16),
            pltpu.VMEM((2, 1024, 1024), BF16),
            pltpu.VMEM((2, 16, 1024), BF16),
            pltpu.VMEM((2, 1024, WIDE), BF16),
            pltpu.VMEM((2, 256, WIDE), BF16),
            pltpu.VMEM((PAIRS, 8, 128), F32),
            pltpu.VMEM((256, 16, 128), BF16),
            pltpu.VMEM((256, 16, 128), BF16),
            pltpu.VMEM((2, 256, 1024), BF16),
            pltpu.VMEM((2, 256, ROWP), F32),
            pltpu.VMEM((2, 256, ROWP), BF16),
            pltpu.VMEM(spectrum_shape, F32),
            pltpu.VMEM((256, 16, 128), BF16),
            pltpu.VMEM((256, 16, 128), BF16),
            pltpu.VMEM((128, 8, 128), F32),
            pltpu.VMEM((8, 128, PAIRS), BF16),
            pltpu.VMEM((PAIRS, PAIRS), BF16),
            pltpu.VMEM((2, 128, 128), F32),
            pltpu.VMEM((NLEV, 8, 128), jnp.int32),
            pltpu.VMEM((NWAVE, 8, 128), jnp.int32),
            pltpu.VMEM((8, 128), jnp.int32),
            pltpu.SMEM((8, 128), jnp.int32),
            dma((2,)), dma, dma, dma, dma, dma, dma, dma, dma, dma, dma((NLEV,)), dma, dma((4,)),
        ],
        compiler_params=pltpu.CompilerParams(
            collective_id=0, has_side_effects=True, vmem_limit_bytes=48 << 20
        ),
        name="exchange",
    )(grid_field, by_row, table, wave_groups, lat_weights.reshape(1, -1), cycle_points, diffusion)
    grid_out, spectrum = pl.pallas_call(
        synthesis,
        out_shape=(
            jax.ShapeDtypeStruct((4, 2, 32, NLON), BF16),
            jax.ShapeDtypeStruct(spectrum_shape, F32),
        ),
        in_specs=[vmem, hbm, hbm],
        out_specs=(hbm, hbm),
        scratch_shapes=[
            pltpu.VMEM((2, 1024, WIDE), BF16),
            pltpu.VMEM((4, 2, 32, NLON), BF16),
            dma((9,)), dma, dma((17,)),
        ],
        compiler_params=pltpu.CompilerParams(vmem_limit_bytes=32 << 20),
        name="synthesis",
    )(back, table, spectrum)
    return spectrum, grid_out


def solution(mesh):
    return jax.shard_map(
        shards,
        mesh=mesh,
        in_specs=(
            P("lev", None, "wave", None),
            P(("wave", "lev"), None, None),
            P(("wave", "lev")),
            P(),
            P(),
            P(),
        ),
        out_specs=(P(("wave", "lev"), None, None, None), P("lev", None, "wave", None)),
        check_vma=False,
    )
```

profile of v0, /device:TPU:2, one launch (start us, length us, event | category | flops | bytes accessed | tf_op | source)
XLA Modules:
  0.0 90.6 jit_solution(9511086450379374977)
XLA Ops:
  0.6 0.0 copy-start.1
  0.6 1.6 %copy-done.1 = bf16[4,2,32,4224]{3,2,1,0:T(8,128)(2,1)S(1)} copy-done((bf16[4,2,32,4224]{3,2,1,0:T(8,128)(2,1)S(1)}, bf16[4,2,32,4224]{3,2,1,0:T(8,128)(2,1)}, u32[]{:S(2)}) %copy-start.1) | copy-done | bytes 2162712
  2.2 0.0 copy-start.2
  2.2 0.7 copy-done.2
  2.9 0.0 copy-start.3
  2.9 0.7 copy-done.3
  3.6 0.0 copy-start.4
  3.6 0.7 copy-done.4
  4.3 0.0 copy-start.5
  4.3 0.7 copy-done.5
  4.9 0.0 copy-start
  4.9 79.3 %exchange.1 = (f32[2,32,2,1025]{3,2,1,0:T(2,128)S(1)}, bf16[2,256,1024]{2,1,0:T(8,128)(2,1)S(1)}) custom-call(bf16[4,2,32,4224]{3,2,1,0:T(8,128)(2,1)S(1)} %copy-done.1, bf16[1025,8,2,128]{3,2,1,0:T(2,128)(2,1)} %bitcast.5, bf16[2,1024,2176]{2,1,0:T(8,128)(2,1)} %constant.2.clone.table_hbm, s32[2]{0:T(128)S(1)} %copy-done.4, f32[1,1024]{1,0:T(1,128)S(1)} %bitcast.4, ...), custom_call_target="tpu_custom_call" | custom-call | tf_op jit(solution)/shard_map/exchange/pallas_call | solution.py:547
  84.3 0.0 copy-done
  84.3 6.3 %synthesis.1 = (bf16[4,2,32,4224]{3,2,1,0:T(8,128)(2,1)}, f32[2,32,2,1025]{3,2,1,0:T(2,128)}) custom-call(bf16[2,256,1024]{2,1,0:T(8,128)(2,1)S(1)} %get-tuple-element.6.back, bf16[2,1024,2176]{2,1,0:T(8,128)(2,1)S(1)} %copy-done, f32[2,32,2,1025]{3,2,1,0:T(2,128)S(1)} %get-tuple-element.7.spec_in), custom_call_target="tpu_custom_call" | custom-call | tf_op jit(solution)/shard_map/synthesis/pallas_call | solution.py:586
Async XLA Ops:
  0.6 1.6 %copy-start.1 = (bf16[4,2,32,4224]{3,2,1,0:T(8,128)(2,1)S(1)}, bf16[4,2,32,4224]{3,2,1,0:T(8,128)(2,1)}, u32[]{:S(2)}) copy-start(bf16[4,2,32,4224]{3,2,1,0:T(8,128)(2,1)} %field_hbm.1) | copy-start | bytes 6488068
  2.2 0.7 copy-start.2
  2.9 0.7 copy-start.3
  3.6 0.7 copy-start.4
  4.3 0.7 copy-start.5
  4.9 79.3 %copy-start = (bf16[2,1024,2176]{2,1,0:T(8,128)(2,1)S(1)}, bf16[2,1024,2176]{2,1,0:T(8,128)(2,1)}, u32[]{:S(2)}) copy-start(bf16[2,1024,2176]{2,1,0:T(8,128)(2,1)} %constant.2.clone.table_hbm) | copy-start | bytes 26738692
where the time goes:
time: 91.7 us; the launch traced here: 90.6 us
  Pallas kernels  85.6 us (93%)
  local copies, waits for them, and re-layouts  4.3 us (5%)
    pallas_call x1, Pallas kernels, shards(): pl.pallas_call(exchange, out_shape=(jax.ShapeDtypeStruct(spectrum_shape,...  79.3 us
    pallas_call x1, Pallas kernels, shards(): pl.pallas_call(synthesis, out_shape=(jax.ShapeDtypeStruct((4, 2, 32, NLON...  6.31 us
    unnamed x12, local copies, waits for them, and re-layouts  4.3 us

commit v1 on v0

--- a/solution.py
+++ b/solution.py
@@ -95,17 +95,29 @@
     )
 
 
+BLOCKS = [(2048, 128)] + [(256 * n, 256) for n in range(8)]
+
+
 def exchange(
-    field_hbm, leg_hbm, table_hbm, ids, weights, points, diffusion,
-    spec_hbm, back,
-    field, raw, leg, last, table, fold, pairs, send_f, recv_f, oper, damp, dope, spec, send_b,
-    recv_b, rows, turned, onehot, column, gat1, gat2, gatv, gats,
-    s_table, s_field, s_leg, s_local, s_spec, s_g1s, s_g1r, s_g2s, s_g2r, s_fs, s_fr, s_bs, s_br,
+    field_hbm, leg_hbm, table_hbm, ids_hbm, weights_hbm, points_hbm, diffusion_hbm,
+    spec, grid,
+    field, raw, leg, last, table, fold, pairs, send_f, recv_f, oper, damp, dope, modes, send_b,
+    recv_b, rows, turned, onehot, column, back, gat1, gat2, gatv, gats, ids, weights, points,
+    diffusion,
+    s_table, s_field, s_leg, s_local, s_small, s_g1s, s_g1r, s_g2s, s_g2r, s_fs, s_fr, s_bs, s_br,
 ):
     w = lax.axis_index("wave")
     l = lax.axis_index("lev")
     me = w * NLEV + l
 
+    small_copies = [
+        pltpu.make_async_copy(a, b, s_small.at[i])
+        for i, (a, b) in enumerate((
+            (ids_hbm, ids), (weights_hbm, weights), (points_hbm, points), (diffusion_hbm, diffusion),
+        ))
+    ]
+    for copy in small_copies:
+        copy.start()
     field_copy = pltpu.make_async_copy(field_hbm, field, s_field)
     field_copy.start()
     table_copies = [
@@ -127,6 +139,8 @@
     lax.fori_loop(1, NLEV, greet_lev, 0)
     lax.fori_loop(1, NWAVE, greet_wave, 0)
 
+    for copy in small_copies:
+        copy.wait()
     a0 = ids[0]
     a1 = ids[1]
     t0 = jnp.where(a0 % 2 == 0, a0 // 2, (WAVES - 1 - a0) // 2)
@@ -202,22 +216,20 @@
         return 4 * pair if p == 0 else 2 * (WAVES - 1) - 4 * pair
 
     def transform(p):
-        for part in range(2):
-            def body(m, c, part=part):
-                first = pl.multiple_of(m * 256, 256)
-                start = pl.multiple_of(part * PAIRS + m * 256, 256)
-                out = lax.dot_general(
-                    table[p, pl.ds(start, 256), :], fold[p], NT, preferred_element_type=F32
-                )
-                twice = twice_wave(p, first + sub_iota((256, 128)))
-                north = jnp.where(twice < band_points[0][0:1, :], out[:, :128], 0.0)
-                south = jnp.where(twice < band_points[1][0:1, :], out[:, 128:], 0.0)
-                scale = band_weights[0:1, :]
-                pairs[pl.ds(first, 256), 2 * p + part, :] = (north + south) * scale
-                pairs[pl.ds(first, 256), 4 + 2 * p + part, :] = (north - south) * scale
-                return c
-
-            lax.fori_loop(0, 2, body, 0)
+        def body(part, c):
+            start = pl.multiple_of(part * PAIRS, PAIRS)
+            out = lax.dot_general(
+                table[p, pl.ds(start, PAIRS), :], fold[p], NT, preferred_element_type=F32
+            )
+            twice = twice_wave(p, sub_iota((PAIRS, 128)))
+            north = jnp.where(twice < band_points[0][0:1, :], out[:, :128], 0.0)
+            south = jnp.where(twice < band_points[1][0:1, :], out[:, 128:], 0.0)
+            scale = band_weights[0:1, :]
+            pairs[:, 2 * p + part, :] = (north + south) * scale
+            pairs[:, 4 + 2 * p + part, :] = (north - south) * scale
+            return c
+
+        lax.fori_loop(0, 2, body, 0)
 
     table_copies[0].wait()
     transform(0)
@@ -258,7 +270,7 @@
         ).start()
         return c
 
-    lax.fori_loop(1, 256, send_forward, 0)
+    lax.fori_loop(1, 256, send_forward, 0, unroll=5)
 
     leg_copy.wait()
 
@@ -300,16 +312,20 @@
 
         lax.fori_loop(0, 32, damp_body, 0)
 
-    for b in range(4):
-        holder = gatv[4 + b:5 + b, :]
-
-        def onehot_body(i, c, b=b, holder=holder):
-            start = pl.multiple_of(i * 128, 128)
-            hit = start + sub_iota((128, 128)) == holder
-            onehot[pl.ds(start, 128), b * 128:(b + 1) * 128] = jnp.where(hit, 1.0, 0.0).astype(BF16)
+    for q in range(4):
+        bases = [2 * lev_from(l, 7 - 2 * q - u) for u in range(2)]
+
+        def onehot_body(b, c, q=q, bases=bases):
+            sub = sub_iota((128, 128))
+            slot = jnp.where(sub < 64, bases[0], bases[1]) + sub % 64 // 2 * 16 + sub % 2
+            for b in range(4):
+                hit = slot == gatv[4 + b:5 + b, :]
+                onehot[q * 128:(q + 1) * 128, b * 128:(b + 1) * 128] = jnp.where(
+                    hit, 1.0, 0.0
+                ).astype(BF16)
             return c
 
-        lax.fori_loop(0, 4, onehot_body, 0)
+        lax.fori_loop(0, 1, onehot_body, 0)
     for h in range(2):
         column[h] = jnp.broadcast_to(band_points[h][0:1, :].astype(F32), (128, 128)).T
 
@@ -372,19 +388,15 @@
             pick(s, a, x, start, 256)
         return c
 
-    lax.fori_loop(0, 4, product, 0)
+    lax.fori_loop(0, 4, product, 0, unroll=4)
     for s, a in enumerate((a0, a1)):
         rhs = jnp.concatenate([last[s]] * 8, axis=0)
         x = lax.dot_general(oper[s], rhs, NT, preferred_element_type=F32)
         pick(s, a, x, 1024, 128)
-    spec_copy = pltpu.make_async_copy(spec, spec_hbm, s_spec)
-    spec_copy.start()
-
-    def inverse(i, c):
-        n = (w // 8 + select8(i, (2, 1, 3, 0))) % 4
+
+    def inverse(n, c):
         start = pl.multiple_of(n * 256, 256)
         sign = jnp.where(sub_iota((1, 8, 256)) < 4, 1.0, -1.0)
-        hemis = []
         for s in range(2):
             x = lax.dot_general(
                 dope[s, :, 0:1024], leg[s, 0:1024, pl.ds(start, 256)], NN,
@@ -393,65 +405,64 @@
             edge = dope[s, :, 1024:ROWP].astype(F32)[:, 0:1]
             x = x + edge * last[s, :, pl.ds(start, 256)].astype(F32)[0:1]
             x = x.reshape(32, 8, 256)
-            hemis.append(x * sign + pltpu.roll(x, 4, 1))
-        for l2 in range(8):
-            for half in range(2):
-                tiles = []
-                for f in range(4):
-                    tiles.append(
-                        jnp.concatenate(
-                            [
-                                hemis[s][4 * l2 + f, :, half * 128:(half + 1) * 128]
-                                for s in range(2)
-                            ],
-                            axis=0,
-                        )
-                    )
-                for u, x in enumerate(swap_lane(*tiles)):
-                    send_b[(8 * n + 4 * half + u) * NLEV + l2] = x.astype(BF16)
+            modes[s, :, :, pl.ds(start, 256)] = x * sign + pltpu.roll(x, 4, 1)
+        return c
+
+    lax.fori_loop(0, 4, inverse, 0, unroll=4)
+
+    def send_group(i, c):
+        l2 = lev_at(l, 7 - i)
+        for block in range(8):
+            lanes = slice(block * 128, (block + 1) * 128)
+            tiles = [
+                jnp.concatenate([modes[s, 4 * l2 + f, :, lanes] for s in range(2)], axis=0)
+                for f in range(4)
+            ]
+            for u, x in enumerate(swap_lane(*tiles)):
+                send_b[(4 * block + u) * NLEV + l2] = x.astype(BF16)
 
         def send_back(m, c):
-            w2 = 8 * n + m % 8
-            l2 = lev_at(l, 7 - m // 8)
+            w2 = wave_at(w, 31 - m)
             d = w2 * NLEV + l2
 
             @pl.when(d != me)
             def _():
                 pltpu.make_async_remote_copy(
                     src_ref=send_b.at[d], dst_ref=recv_b.at[me], send_sem=s_bs,
-                    recv_sem=s_br.at[w // 8], device_id=(w2, l2), device_id_type=MESH,
+                    recv_sem=s_br.at[l], device_id=(w2, l2), device_id_type=MESH,
                 ).start()
 
             return c
 
-        lax.fori_loop(0, 64, send_back, 0)
-        return c
-
-    lax.fori_loop(0, 4, inverse, 0)
+        lax.fori_loop(0, 32, send_back, 0)
+        return c
+
+    lax.fori_loop(0, 8, send_group, 0)
     recv_b[me] = send_b[me]
 
-    def returned(i, c):
-        n = (w // 8 + 4 - select8(i, (2, 1, 3, 0))) % 4
-
-        def landed(count):
-            pltpu.make_async_remote_copy(
-                src_ref=send_b.at[pl.ds(0, count)], dst_ref=recv_b.at[pl.ds(0, count)],
-                send_sem=s_bs, recv_sem=s_br.at[n], device_id=(w, l), device_id_type=MESH,
-            ).wait_recv()
-
-        @pl.when(i == 3)
-        def _():
-            landed(63)
-
-        @pl.when(i != 3)
-        def _():
-            landed(64)
-
-        for d in range(64):
-            both = recv_b[64 * n + d].astype(F32)
-            rows[2 * d] = both[0:8]
-            rows[2 * d + 1] = both[8:16]
-        lanes = pl.multiple_of(n * 128, 128)
+    def returned(q, c):
+        for u in range(2):
+            src = lev_from(l, 7 - 2 * q - u)
+
+            def landed(count, src=src):
+                pltpu.make_async_remote_copy(
+                    src_ref=send_b.at[pl.ds(0, count)], dst_ref=recv_b.at[pl.ds(0, count)],
+                    send_sem=s_bs, recv_sem=s_br.at[src], device_id=(w, l), device_id_type=MESH,
+                ).wait_recv()
+
+            @pl.when(src == l)
+            def _():
+                landed(NWAVE - 1)
+
+            @pl.when(src != l)
+            def _():
+                landed(NWAVE)
+
+            for v in range(NWAVE):
+                both = recv_b[v * NLEV + src].astype(F32)
+                rows[64 * u + 2 * v] = both[0:8]
+                rows[64 * u + 2 * v + 1] = both[8:16]
+        lanes = pl.multiple_of(q * 128, 128)
         for j in range(8):
             turned[j, :, pl.ds(lanes, 128)] = rows[:, j, :].T.astype(BF16)
         return c
@@ -470,58 +481,20 @@
                 x = x * (jnp.where(twice == 0, 1.0, 2.0) if p == 0 else 2.0)
                 back[p, h * 128:(h + 1) * 128, r * PAIRS:(r + 1) * PAIRS] = x.astype(BF16)
 
-    spec_copy.wait()
-    pltpu.make_async_remote_copy(
-        src_ref=send_f.at[pl.ds(0, 255)], dst_ref=recv_f.at[pl.ds(0, 255)], send_sem=s_fs,
-        recv_sem=s_g1r, device_id=(w, l), device_id_type=MESH,
-    ).wait_send()
-    pltpu.make_async_remote_copy(
-        src_ref=send_b.at[pl.ds(0, 255)], dst_ref=recv_b.at[pl.ds(0, 255)], send_sem=s_bs,
-        recv_sem=s_g1r, device_id=(w, l), device_id_type=MESH,
-    ).wait_send()
-
-
-BLOCKS = [(0, 2048, 128)] + [(1 + n, 256 * n, 256) for n in range(8)]
-
-
-def synthesis(
-    back, table_hbm, spec_in, grid_hbm, spec_out, table, outv, s_table, s_spec, s_out
-):
-    copies = []
-    for i, start, width in BLOCKS:
-        copies.append(
-            pltpu.make_async_copy(
-                table_hbm.at[:, :, pl.ds(start, width)], table.at[:, :, pl.ds(start, width)],
-                s_table.at[i],
-            )
-        )
-        copies[-1].start()
-    spec_copy = pltpu.make_async_copy(spec_in, spec_out, s_spec)
-    spec_copy.start()
-    outs = []
-
     def write(x, start, width):
         for h in range(2):
             for f in range(4):
                 row = h * 128 + f * 32
-                outv[f, h, :, start:start + width] = x[row:row + 32].astype(BF16)
-        outs.append(
-            pltpu.make_async_copy(
-                outv.at[:, :, :, pl.ds(start, width)], grid_hbm.at[:, :, :, pl.ds(start, width)],
-                s_out.at[len(outs)],
-            )
-        )
-        outs[-1].start()
+                grid[f, h, :, start:start + width] = x[row:row + 32].astype(BF16)
 
     tail = None
     before = None
-    for i, start, width in BLOCKS:
-        copies[i].wait()
+    for start, width in BLOCKS:
         x = jnp.dot(back[0], table[0, :, start:start + width], preferred_element_type=F32)
         y = jnp.dot(back[1], table[1, :, start:start + width], preferred_element_type=F32)
         total = x + y
         differ = pltpu.roll(x - y, 64, 1)
-        if i == 0:
+        if width == 128:
             tail = differ
             before = total
         else:
@@ -531,27 +504,31 @@
             write(jnp.concatenate([edge, differ[:, 128:]], axis=1), 2048 + start, 256)
             before = differ[:, :128]
     write(jnp.where(lane_iota((256, 128)) < 64, before, tail), 4096, 128)
-    for copy in outs:
-        copy.wait()
-    spec_copy.wait()
+
+    pltpu.make_async_remote_copy(
+        src_ref=send_f.at[pl.ds(0, 255)], dst_ref=recv_f.at[pl.ds(0, 255)], send_sem=s_fs,
+        recv_sem=s_g1r, device_id=(w, l), device_id_type=MESH,
+    ).wait_send()
+    pltpu.make_async_remote_copy(
+        src_ref=send_b.at[pl.ds(0, 255)], dst_ref=recv_b.at[pl.ds(0, 255)], send_sem=s_bs,
+        recv_sem=s_g1r, device_id=(w, l), device_id_type=MESH,
+    ).wait_send()
 
 
 def shards(grid_field, legendre, wave_groups, lat_weights, cycle_points, diffusion):
     dma = pltpu.SemaphoreType.DMA
     vmem = pl.BlockSpec(memory_space=pltpu.VMEM)
-    smem = pl.BlockSpec(memory_space=pltpu.SMEM)
-    hbm = pl.BlockSpec(memory_space=pl.ANY)
+    hbm = pl.BlockSpec(memory_space=pltpu.HBM)
     table = jnp.asarray(basis_tables())
     by_row = legendre.reshape(2, ROWS, 8, 128).transpose(1, 2, 0, 3)
-    spectrum_shape = (2, 32, 2, ROWS)
-    spectrum, back = pl.pallas_call(
+    return pl.pallas_call(
         exchange,
         out_shape=(
-            jax.ShapeDtypeStruct(spectrum_shape, F32),
-            jax.ShapeDtypeStruct((2, 256, 1024), BF16),
+            pltpu.VMEM((2, 32, 2, ROWS), F32),
+            pltpu.VMEM((4, 2, 32, NLON), BF16),
         ),
-        in_specs=[hbm, hbm, hbm, smem, vmem, vmem, smem],
-        out_specs=(hbm, vmem),
+        in_specs=[hbm] * 7,
+        out_specs=(vmem, vmem),
         scratch_shapes=[
             pltpu.VMEM((4, 2, 32, NLON), BF16),
             pltpu.VMEM((ROWS, 8, 2, 128), BF16),
@@ -565,41 +542,30 @@
             pltpu.VMEM((2, 256, 1024), BF16),
             pltpu.VMEM((2, 256, ROWP), F32),
             pltpu.VMEM((2, 256, ROWP), BF16),
-            pltpu.VMEM(spectrum_shape, F32),
+            pltpu.VMEM((2, 32, 8, 1024), F32),
             pltpu.VMEM((256, 16, 128), BF16),
             pltpu.VMEM((256, 16, 128), BF16),
             pltpu.VMEM((128, 8, 128), F32),
             pltpu.VMEM((8, 128, PAIRS), BF16),
             pltpu.VMEM((PAIRS, PAIRS), BF16),
             pltpu.VMEM((2, 128, 128), F32),
+            pltpu.VMEM((2, 256, 1024), BF16),
             pltpu.VMEM((NLEV, 8, 128), jnp.int32),
             pltpu.VMEM((NWAVE, 8, 128), jnp.int32),
             pltpu.VMEM((8, 128), jnp.int32),
             pltpu.SMEM((8, 128), jnp.int32),
-            dma((2,)), dma, dma, dma, dma, dma, dma, dma, dma, dma, dma((NLEV,)), dma, dma((4,)),
+            pltpu.SMEM((2,), jnp.int32),
+            pltpu.VMEM((1, 1024), F32),
+            pltpu.VMEM((2, 1024), jnp.int32),
+            pltpu.SMEM((32,), F32),
+            dma((2,)), dma, dma, dma, dma((4,)), dma, dma, dma, dma, dma, dma((NLEV,)), dma,
+            dma((NLEV,)),
         ],
         compiler_params=pltpu.CompilerParams(
-            collective_id=0, has_side_effects=True, vmem_limit_bytes=48 << 20
+            collective_id=0, has_side_effects=True, vmem_limit_bytes=56 << 20
         ),
         name="exchange",
     )(grid_field, by_row, table, wave_groups, lat_weights.reshape(1, -1), cycle_points, diffusion)
-    grid_out, spectrum = pl.pallas_call(
-        synthesis,
-        out_shape=(
-            jax.ShapeDtypeStruct((4, 2, 32, NLON), BF16),
-            jax.ShapeDtypeStruct(spectrum_shape, F32),
-        ),
-        in_specs=[vmem, hbm, hbm],
-        out_specs=(hbm, hbm),
-        scratch_shapes=[
-            pltpu.VMEM((2, 1024, WIDE), BF16),
-            pltpu.VMEM((4, 2, 32, NLON), BF16),
-            dma((9,)), dma, dma((17,)),
-        ],
-        compiler_params=pltpu.CompilerParams(vmem_limit_bytes=32 << 20),
-        name="synthesis",
-    )(back, table, spectrum)
-    return spectrum, grid_out
 
 
 def solution(mesh):

time: 91.7 us -> 83 us (0.905)
  Pallas kernels: 85.6 us -> 79.7 us
  local copies, waits for them, and re-layouts: 4.3 us -> 2.16 us
    pallas_call x2 -> x1, Pallas kernels: 85.6 us -> 79.7 us  [shards(): pl.pallas_call(exchange, out_shape=(pltpu.VMEM((2, 32, 2, ROWS), F32), pl...]
    unnamed x12 -> x2, local copies, waits for them, and re-layouts: 4.3 us -> 2.16 us
where the time goes in v1:
time: 83 us; the launch traced here: 82.5 us
  Pallas kernels  79.7 us (96%)
  local copies, waits for them, and re-layouts  2.16 us (3%)
    pallas_call x1, Pallas kernels, shards(): pl.pallas_call(exchange, out_shape=(pltpu.VMEM((2, 32, 2, ROWS), F32), pl...  79.7 us
    unnamed x2, local copies, waits for them, and re-layouts  2.16 us

profile of v1, /device:TPU:2, one launch (start us, length us, event | category | flops | bytes accessed | tf_op | source)
XLA Modules:
  0.0 82.5 jit_solution(5664377181408876179)
XLA Ops:
  0.6 79.7 %exchange.1 = (f32[2,32,2,1025]{3,2,1,0:T(2,128)S(1)}, bf16[4,2,32,4224]{3,2,1,0:T(8,128)(2,1)S(1)}) custom-call(bf16[4,2,32,4224]{3,2,1,0:T(8,128)(2,1)} %field_hbm.1, bf16[1025,8,2,128]{3,2,1,0:T(2,128)(2,1)} %bitcast.4, bf16[2,1024,2176]{2,1,0:T(8,128)(2,1)} %constant.2.clone.table_hbm, s32[2]{0:T(128)} %ids_hbm.1, f32[1,1024]{1,0:T(1,128)} %bitcast.5, ...), custom_call_target="tpu_custom_call" | custom-call | tf_op jit(solution)/shard_map/exchange/pallas_call | solution.py:524
  80.3 0.8 copy.11
  81.1 1.3 %copy.12 = bf16[4,2,32,4224]{3,2,1,0:T(8,128)(2,1)} copy(bf16[4,2,32,4224]{3,2,1,0:T(8,128)(2,1)S(1)} %get-tuple-element.3) | data formatting | bytes 4325376

commit v2 on v1

--- a/solution.py
+++ b/solution.py
@@ -288,6 +288,10 @@
         for s in range(2):
             last[s, :, ch * 128:(ch + 1) * 128] = jnp.broadcast_to(x[s:s + 1], (16, 128)).astype(BF16)
 
+    def field_of(g):
+        core = (l + 1 + g // 16) % 2
+        return (g // 4 % 4 * 2 + core) * 4 + g % 4
+
     def chosen(a, base, width):
         sub = sub_iota((8, width))
         k = base + lane_iota((8, width))
@@ -307,7 +311,7 @@
 
         def damp_body(f, c, s=s, squared=squared, one=one):
             row = pl.multiple_of(f * 8, 8)
-            damp[s, pl.ds(row, 8), :] = one / (1.0 + diffusion[f] * squared)
+            damp[s, pl.ds(row, 8), :] = one / (1.0 + diffusion[field_of(f)] * squared)
             return c
 
         lax.fori_loop(0, 32, damp_body, 0)
@@ -347,11 +351,11 @@
             landed(NWAVE)
 
         for block in range(8):
-            tiles = [recv_f[(4 * block + i) * NLEV + src].astype(F32) for i in range(4)]
+            tiles = [recv_f[(4 * block + v) * NLEV + src].astype(F32) for v in range(4)]
             by_field = swap_lane(*tiles)
             for s in range(2):
                 for pair in range(2):
-                    row = pl.multiple_of(src * 32 + pair * 16, 16)
+                    row = pl.multiple_of(i // 4 * 128 + src // 2 * 32 + pair * 16, 16)
                     oper[s, pl.ds(row, 16), block * 128:(block + 1) * 128] = jnp.concatenate(
                         [
                             by_field[2 * pair][8 * s:8 * s + 8],
@@ -361,61 +365,67 @@
                     ).astype(BF16)
         return c
 
-    lax.fori_loop(0, 8, arrive, 0)
-
-    def pick(s, a, x, start, width):
+    def pick(half, s, a, x, start, width):
         sel, _ = chosen(a, start, width)
         lanes = pl.ds(start, width)
-        for i in range(16):
+        for i in range(8):
             damped = []
-            for f in (2 * i, 2 * i + 1):
-                y = jnp.where(sel, x[8 * f:8 * f + 8], 0.0)
+            for g in (2 * i, 2 * i + 1):
+                y = jnp.where(sel, x[8 * g:8 * g + 8], 0.0)
                 y = y + pltpu.roll(y, 4, 0)
                 y = y + pltpu.roll(y, 2, 0)
+                f = field_of(16 * half + g)
                 if width == 128:
                     spec[s, f, :, 1024:ROWS] = y[0:2, 0:1]
                 else:
                     spec[s, f, :, lanes] = y[0:2]
-                damped.append(y * damp[s, 8 * f:8 * f + 8, lanes])
-            dope[s, 16 * i:16 * i + 16, lanes] = jnp.concatenate(damped, axis=0).astype(BF16)
-
-    def product(n, c):
-        start = pl.multiple_of(n * 256, 256)
+                row = 128 * half + 8 * g
+                damped.append(y * damp[s, row:row + 8, lanes])
+            row = 128 * half + 16 * i
+            dope[s, row:row + 16, lanes] = jnp.concatenate(damped, axis=0).astype(BF16)
+
+    def legendre_step(half):
+        mine = slice(128 * half, 128 * half + 128)
+
+        def product(n, c):
+            start = pl.multiple_of(n * 256, 256)
+            for s, a in enumerate((a0, a1)):
+                x = lax.dot_general(
+                    oper[s, mine], leg[s, pl.ds(start, 256), :], NT, preferred_element_type=F32
+                )
+                pick(half, s, a, x, start, 256)
+            return c
+
+        lax.fori_loop(0, 4, product, 0, unroll=2)
         for s, a in enumerate((a0, a1)):
-            x = lax.dot_general(
-                oper[s], leg[s, pl.ds(start, 256), :], NT, preferred_element_type=F32
-            )
-            pick(s, a, x, start, 256)
-        return c
-
-    lax.fori_loop(0, 4, product, 0, unroll=4)
-    for s, a in enumerate((a0, a1)):
-        rhs = jnp.concatenate([last[s]] * 8, axis=0)
-        x = lax.dot_general(oper[s], rhs, NT, preferred_element_type=F32)
-        pick(s, a, x, 1024, 128)
-
-    def inverse(n, c):
-        start = pl.multiple_of(n * 256, 256)
-        sign = jnp.where(sub_iota((1, 8, 256)) < 4, 1.0, -1.0)
-        for s in range(2):
-            x = lax.dot_general(
-                dope[s, :, 0:1024], leg[s, 0:1024, pl.ds(start, 256)], NN,
-                preferred_element_type=F32,
-            )
-            edge = dope[s, :, 1024:ROWP].astype(F32)[:, 0:1]
-            x = x + edge * last[s, :, pl.ds(start, 256)].astype(F32)[0:1]
-            x = x.reshape(32, 8, 256)
-            modes[s, :, :, pl.ds(start, 256)] = x * sign + pltpu.roll(x, 4, 1)
-        return c
-
-    lax.fori_loop(0, 4, inverse, 0, unroll=4)
+            rhs = jnp.concatenate([last[s]] * 8, axis=0)
+            x = lax.dot_general(oper[s, mine], rhs, NT, preferred_element_type=F32)
+            pick(half, s, a, x, 1024, 128)
+
+        def inverse(n, c):
+            start = pl.multiple_of(n * 256, 256)
+            sign = jnp.where(sub_iota((1, 8, 256)) < 4, 1.0, -1.0)
+            for s in range(2):
+                x = lax.dot_general(
+                    dope[s, mine, 0:1024], leg[s, 0:1024, pl.ds(start, 256)], NN,
+                    preferred_element_type=F32,
+                )
+                edge = dope[s, mine, 1024:ROWP].astype(F32)[:, 0:1]
+                x = x + edge * last[s, :, pl.ds(start, 256)].astype(F32)[0:1]
+                x = x.reshape(16, 8, 256)
+                modes[s, 16 * half:16 * half + 16, :, pl.ds(start, 256)] = (
+                    x * sign + pltpu.roll(x, 4, 1)
+                )
+            return c
+
+        lax.fori_loop(0, 4, inverse, 0, unroll=2)
 
     def send_group(i, c):
         l2 = lev_at(l, 7 - i)
         for block in range(8):
             lanes = slice(block * 128, (block + 1) * 128)
             tiles = [
-                jnp.concatenate([modes[s, 4 * l2 + f, :, lanes] for s in range(2)], axis=0)
+                jnp.concatenate([modes[s, i // 4 * 16 + l2 // 2 * 4 + f, :, lanes] for s in range(2)], axis=0)
                 for f in range(4)
             ]
             for u, x in enumerate(swap_lane(*tiles)):
@@ -437,7 +447,10 @@
         lax.fori_loop(0, 32, send_back, 0)
         return c
 
-    lax.fori_loop(0, 8, send_group, 0)
+    for half in range(2):
+        lax.fori_loop(4 * half, 4 * half + 4, arrive, 0)
+        legendre_step(half)
+        lax.fori_loop(4 * half, 4 * half + 4, send_group, 0)
     recv_b[me] = send_b[me]
 
     def returned(q, c):

time: 83 us -> 81.2 us (0.978)
  Pallas kernels: 79.7 us -> 78.3 us
    pallas_call x1, Pallas kernels: 79.7 us -> 78.3 us  [shards(): pl.pallas_call(exchange, out_shape=(pltpu.VMEM((2, 32, 2, ROWS), F32), pl...]
where the time goes in v2:
time: 81.2 us; the launch traced here: 81.1 us
  Pallas kernels  78.3 us (96%)
  local copies, waits for them, and re-layouts  2.16 us (3%)
    pallas_call x1, Pallas kernels, shards(): pl.pallas_call(exchange, out_shape=(pltpu.VMEM((2, 32, 2, ROWS), F32), pl...  78.3 us
    unnamed x2, local copies, waits for them, and re-layouts  2.16 us

profile of v2, /device:TPU:2, one launch (start us, length us, event | category | flops | bytes accessed | tf_op | source)
XLA Modules:
  0.0 81.1 jit_solution(4795337019536871496)
XLA Ops:
  0.6 78.3 %exchange.1 = (f32[2,32,2,1025]{3,2,1,0:T(2,128)S(1)}, bf16[4,2,32,4224]{3,2,1,0:T(8,128)(2,1)S(1)}) custom-call(bf16[4,2,32,4224]{3,2,1,0:T(8,128)(2,1)} %field_hbm.1, bf16[1025,8,2,128]{3,2,1,0:T(2,128)(2,1)} %bitcast.4, bf16[2,1024,2176]{2,1,0:T(8,128)(2,1)} %constant.2.clone.table_hbm, s32[2]{0:T(128)} %ids_hbm.1, f32[1,1024]{1,0:T(1,128)} %bitcast.5, ...), custom_call_target="tpu_custom_call" | custom-call | tf_op jit(solution)/shard_map/exchange/pallas_call | solution.py:537
  78.9 0.8 %copy.11 = f32[2,32,2,1025]{3,2,1,0:T(2,128)} copy(f32[2,32,2,1025]{3,2,1,0:T(2,128)S(1)} %get-tuple-element.2) | data formatting | bytes 1049600
  79.7 1.3 %copy.12 = bf16[4,2,32,4224]{3,2,1,0:T(8,128)(2,1)} copy(bf16[4,2,32,4224]{3,2,1,0:T(8,128)(2,1)S(1)} %get-tuple-element.3) | data formatting | bytes 4325376

commit v3 on v2

--- a/solution.py
+++ b/solution.py
@@ -123,7 +123,6 @@
     table_copies = [
         pltpu.make_async_copy(table_hbm.at[p], table.at[p], s_table.at[p]) for p in range(2)
     ]
-    table_copies[0].start()
     leg_copy = pltpu.make_async_copy(leg_hbm, raw, s_leg)
 
     barrier = pltpu.get_barrier_semaphore()
@@ -138,6 +137,7 @@
 
     lax.fori_loop(1, NLEV, greet_lev, 0)
     lax.fori_loop(1, NWAVE, greet_wave, 0)
+    table_copies[0].start()
 
     for copy in small_copies:
         copy.wait()
@@ -145,11 +145,9 @@
     a1 = ids[1]
     t0 = jnp.where(a0 % 2 == 0, a0 // 2, (WAVES - 1 - a0) // 2)
     t1 = jnp.where(a1 % 2 == 0, a1 // 2, (WAVES - 1 - a1) // 2)
-    flat = sub_iota((8, 128)) * 128 + lane_iota((8, 128))
-    tile = jnp.where(flat == 2 * me, t0, 0) + jnp.where(flat == 2 * me + 1, t1, 0)
-    tile = tile + jnp.where(flat == PAIRS + t0, 2 * me, 0)
-    tile = tile + jnp.where(flat == PAIRS + t1, 2 * me + 1, 0)
-    gat1[l] = tile
+    lane = lane_iota((1, 128))
+    place = 2 * me % 128
+    gat1[l] = jnp.where(lane == place, t0, 0) + jnp.where(lane == place + 1, t1, 0)
 
     band = pl.multiple_of(w // 4 * 128, 128)
     turn = (4 - w % 4) % 4 * 32
@@ -229,7 +227,7 @@
             pairs[:, 4 + 2 * p + part, :] = (north - south) * scale
             return c
 
-        lax.fori_loop(0, 2, body, 0)
+        lax.fori_loop(0, 2, body, 0, unroll=2)
 
     table_copies[0].wait()
     transform(0)
@@ -243,10 +241,11 @@
     )
     g2.wait_send()
     g2.wait_recv()
-    total = gat2[0]
-    for i in range(1, NWAVE):
-        total = total + gat2[i]
-    gatv[...] = jnp.clip(total, 0, PAIRS - 1)
+    for r in range(4):
+        total = gat2[8 * r]
+        for i in range(1, 8):
+            total = total + gat2[8 * r + i]
+        gatv[r:r + 1, :] = jnp.clip(total, 0, PAIRS - 1)
     ids_copy = pltpu.make_async_copy(gatv, gats, s_local)
     ids_copy.start()
     ids_copy.wait()
@@ -316,6 +315,16 @@
 
         lax.fori_loop(0, 32, damp_body, 0)
 
+    holders = [jnp.zeros((1, 128), F32)] * 4
+    for r in range(4):
+        held = jnp.broadcast_to(gatv[r:r + 1, :].astype(F32), (128, 128)).T
+        slot = (128 * r + sub_iota((128, 128))).astype(F32)
+        for b in range(4):
+            pair = (128 * b + lane_iota((128, 128))).astype(F32)
+            hit = jnp.where(held == pair, slot, 0.0)
+            holders[b] = holders[b] + jnp.sum(hit, axis=0, keepdims=True)
+    holders = [holder.astype(jnp.int32) for holder in holders]
+
     for q in range(4):
         bases = [2 * lev_from(l, 7 - 2 * q - u) for u in range(2)]
 
@@ -323,7 +332,7 @@
             sub = sub_iota((128, 128))
             slot = jnp.where(sub < 64, bases[0], bases[1]) + sub % 64 // 2 * 16 + sub % 2
             for b in range(4):
-                hit = slot == gatv[4 + b:5 + b, :]
+                hit = slot == holders[b]
                 onehot[q * 128:(q + 1) * 128, b * 128:(b + 1) * 128] = jnp.where(
                     hit, 1.0, 0.0
                 ).astype(BF16)
@@ -563,10 +572,10 @@
             pltpu.VMEM((PAIRS, PAIRS), BF16),
             pltpu.VMEM((2, 128, 128), F32),
             pltpu.VMEM((2, 256, 1024), BF16),
-            pltpu.VMEM((NLEV, 8, 128), jnp.int32),
-            pltpu.VMEM((NWAVE, 8, 128), jnp.int32),
-            pltpu.VMEM((8, 128), jnp.int32),
-            pltpu.SMEM((8, 128), jnp.int32),
+            pltpu.VMEM((NLEV, 1, 128), jnp.int32),
+            pltpu.VMEM((NWAVE, 1, 128), jnp.int32),
+            pltpu.VMEM((4, 128), jnp.int32),
+            pltpu.SMEM((4, 128), jnp.int32),
             pltpu.SMEM((2,), jnp.int32),
             pltpu.VMEM((1, 1024), F32),
             pltpu.VMEM((2, 1024), jnp.int32),

time: 81.2 us -> 79 us (0.973)
  Pallas kernels: 78.3 us -> 76.1 us
    pallas_call x1, Pallas kernels: 78.3 us -> 76.1 us  [shards(): pl.pallas_call(exchange, out_shape=(pltpu.VMEM((2, 32, 2, ROWS), F32), pl...]
where the time goes in v3:
time: 79 us; the launch traced here: 78.9 us
  Pallas kernels  76.1 us (96%)
  local copies, waits for them, and re-layouts  2.16 us (3%)
    pallas_call x1, Pallas kernels, shards(): pl.pallas_call(exchange, out_shape=(pltpu.VMEM((2, 32, 2, ROWS), F32), pl...  76.1 us
    unnamed x2, local copies, waits for them, and re-layouts  2.16 us

profile of v3, /device:TPU:2, one launch (start us, length us, event | category | flops | bytes accessed | tf_op | source)
XLA Modules:
  0.0 78.9 jit_solution(17761122960599458831)
XLA Ops:
  0.6 76.1 %exchange.1 = (f32[2,32,2,1025]{3,2,1,0:T(2,128)S(1)}, bf16[4,2,32,4224]{3,2,1,0:T(8,128)(2,1)S(1)}) custom-call(bf16[4,2,32,4224]{3,2,1,0:T(8,128)(2,1)} %field_hbm.1, bf16[1025,8,2,128]{3,2,1,0:T(2,128)(2,1)} %bitcast.4, bf16[2,1024,2176]{2,1,0:T(8,128)(2,1)} %constant.2.clone.table_hbm, s32[2]{0:T(128)} %ids_hbm.1, f32[1,1024]{1,0:T(1,128)} %bitcast.5, ...), custom_call_target="tpu_custom_call" | custom-call | tf_op jit(solution)/shard_map/exchange/pallas_call | solution.py:546
  76.8 0.8 %copy.11 = f32[2,32,2,1025]{3,2,1,0:T(2,128)} copy(f32[2,32,2,1025]{3,2,1,0:T(2,128)S(1)} %get-tuple-element.2) | data formatting | bytes 1049600
  77.6 1.3 %copy.12 = bf16[4,2,32,4224]{3,2,1,0:T(8,128)(2,1)} copy(bf16[4,2,32,4224]{3,2,1,0:T(8,128)(2,1)S(1)} %get-tuple-element.3) | data formatting | bytes 4325376

commit v4 on v3

--- a/solution.py
+++ b/solution.py
@@ -61,10 +61,14 @@
     return (l // 2 + 4 - dx) % 4 * 2 + (l % 2 + dc) % 2
 
 
-def wave_at(w, index):
-    dz = select8(index % 8, Z_ORDER)
-    dy = select8(index // 8, Y_ORDER)
-    return (w // 4 + dz) % 8 * 4 + (w % 4 + dy) % 4
+def target(w, l, dc, m):
+    z = m % 8
+    k = m // 8
+    dz = select8(z, Z_ORDER)
+    dx = select8((k + z) % 4, Y_ORDER)
+    dy = select8((k // 4 + z // 2) % 4, Y_ORDER)
+    w2 = (w // 4 + dz) % 8 * 4 + (w % 4 + dy) % 4
+    return w2, (l // 2 + dx) % 4 * 2 + (l % 2 + dc) % 2
 
 
 def sub_iota(shape):
@@ -259,8 +263,7 @@
 
     def send_forward(i, c):
         j = 256 - i
-        w2 = wave_at(w, j % NWAVE)
-        l2 = lev_at(l, j // NWAVE)
+        w2, l2 = target(w, l, j // 128, j % 128)
         d = w2 * NLEV + l2
         send_f[d] = packed(d)
         pltpu.make_async_remote_copy(
@@ -314,33 +317,6 @@
             return c
 
         lax.fori_loop(0, 32, damp_body, 0)
-
-    holders = [jnp.zeros((1, 128), F32)] * 4
-    for r in range(4):
-        held = jnp.broadcast_to(gatv[r:r + 1, :].astype(F32), (128, 128)).T
-        slot = (128 * r + sub_iota((128, 128))).astype(F32)
-        for b in range(4):
-            pair = (128 * b + lane_iota((128, 128))).astype(F32)
-            hit = jnp.where(held == pair, slot, 0.0)
-            holders[b] = holders[b] + jnp.sum(hit, axis=0, keepdims=True)
-    holders = [holder.astype(jnp.int32) for holder in holders]
-
-    for q in range(4):
-        bases = [2 * lev_from(l, 7 - 2 * q - u) for u in range(2)]
-
-        def onehot_body(b, c, q=q, bases=bases):
-            sub = sub_iota((128, 128))
-            slot = jnp.where(sub < 64, bases[0], bases[1]) + sub % 64 // 2 * 16 + sub % 2
-            for b in range(4):
-                hit = slot == holders[b]
-                onehot[q * 128:(q + 1) * 128, b * 128:(b + 1) * 128] = jnp.where(
-                    hit, 1.0, 0.0
-                ).astype(BF16)
-            return c
-
-        lax.fori_loop(0, 1, onehot_body, 0)
-    for h in range(2):
-        column[h] = jnp.broadcast_to(band_points[h][0:1, :].astype(F32), (128, 128)).T
 
     def arrive(i, c):
         src = lev_from(l, 7 - i)
@@ -439,9 +415,15 @@
             ]
             for u, x in enumerate(swap_lane(*tiles)):
                 send_b[(4 * block + u) * NLEV + l2] = x.astype(BF16)
-
-        def send_back(m, c):
-            w2 = wave_at(w, 31 - m)
+        return c
+
+    for half in range(2):
+        lax.fori_loop(4 * half, 4 * half + 4, arrive, 0)
+        legendre_step(half)
+        lax.fori_loop(4 * half, 4 * half + 4, send_group, 0)
+
+        def send_back(m, c, half=half):
+            w2, l2 = target(w, l, 1 - half, 127 - m)
             d = w2 * NLEV + l2
 
             @pl.when(d != me)
@@ -453,14 +435,35 @@
 
             return c
 
-        lax.fori_loop(0, 32, send_back, 0)
-        return c
-
-    for half in range(2):
-        lax.fori_loop(4 * half, 4 * half + 4, arrive, 0)
-        legendre_step(half)
-        lax.fori_loop(4 * half, 4 * half + 4, send_group, 0)
+        lax.fori_loop(0, 128, send_back, 0)
     recv_b[me] = send_b[me]
+
+    holders = [jnp.zeros((1, 128), F32)] * 4
+    for r in range(4):
+        held = jnp.broadcast_to(gatv[r:r + 1, :].astype(F32), (128, 128)).T
+        slot = (128 * r + sub_iota((128, 128))).astype(F32)
+        for b in range(4):
+            pair = (128 * b + lane_iota((128, 128))).astype(F32)
+            hit = jnp.where(held == pair, slot, 0.0)
+            holders[b] = holders[b] + jnp.sum(hit, axis=0, keepdims=True)
+    holders = [holder.astype(jnp.int32) for holder in holders]
+
+    for q in range(4):
+        bases = [2 * lev_from(l, 7 - 2 * q - u) for u in range(2)]
+
+        def onehot_body(b, c, q=q, bases=bases):
+            sub = sub_iota((128, 128))
+            slot = jnp.where(sub < 64, bases[0], bases[1]) + sub % 64 // 2 * 16 + sub % 2
+            for b in range(4):
+                hit = slot == holders[b]
+                onehot[q * 128:(q + 1) * 128, b * 128:(b + 1) * 128] = jnp.where(
+                    hit, 1.0, 0.0
+                ).astype(BF16)
+            return c
+
+        lax.fori_loop(0, 1, onehot_body, 0)
+    for h in range(2):
+        column[h] = jnp.broadcast_to(band_points[h][0:1, :].astype(F32), (128, 128)).T
 
     def returned(q, c):
         for u in range(2):

time: 79 us -> 83.5 us (1.057)
  Pallas kernels: 76.1 us -> 80.6 us
    pallas_call x1, Pallas kernels: 76.1 us -> 80.6 us  [shards(): pl.pallas_call(exchange, out_shape=(pltpu.VMEM((2, 32, 2, ROWS), F32), pl...]
where the time goes in v4:
time: 83.5 us; the launch traced here: 83.4 us
  Pallas kernels  80.6 us (97%)
  local copies, waits for them, and re-layouts  2.16 us (3%)
    pallas_call x1, Pallas kernels, shards(): pl.pallas_call(exchange, out_shape=(pltpu.VMEM((2, 32, 2, ROWS), F32), pl...  80.6 us
    unnamed x2, local copies, waits for them, and re-layouts  2.16 us

profile of v4, /device:TPU:2, one launch (start us, length us, event | category | flops | bytes accessed | tf_op | source)
XLA Modules:
  0.0 83.4 jit_solution(3514718203640100489)
XLA Ops:
  0.6 80.6 %exchange.1 = (f32[2,32,2,1025]{3,2,1,0:T(2,128)S(1)}, bf16[4,2,32,4224]{3,2,1,0:T(8,128)(2,1)S(1)}) custom-call(bf16[4,2,32,4224]{3,2,1,0:T(8,128)(2,1)} %field_hbm.1, bf16[1025,8,2,128]{3,2,1,0:T(2,128)(2,1)} %bitcast.4, bf16[2,1024,2176]{2,1,0:T(8,128)(2,1)} %constant.2.clone.table_hbm, s32[2]{0:T(128)} %ids_hbm.1, f32[1,1024]{1,0:T(1,128)} %bitcast.5, ...), custom_call_target="tpu_custom_call" | custom-call | tf_op jit(solution)/shard_map/exchange/pallas_call | solution.py:549
  81.2 0.8 copy.11
  82.0 1.3 %copy.12 = bf16[4,2,32,4224]{3,2,1,0:T(8,128)(2,1)} copy(bf16[4,2,32,4224]{3,2,1,0:T(8,128)(2,1)S(1)} %get-tuple-element.3) | data formatting | bytes 4325376

commit v5 on v4

--- a/solution.py
+++ b/solution.py
@@ -61,14 +61,10 @@
     return (l // 2 + 4 - dx) % 4 * 2 + (l % 2 + dc) % 2
 
 
-def target(w, l, dc, m):
-    z = m % 8
-    k = m // 8
-    dz = select8(z, Z_ORDER)
-    dx = select8((k + z) % 4, Y_ORDER)
-    dy = select8((k // 4 + z // 2) % 4, Y_ORDER)
-    w2 = (w // 4 + dz) % 8 * 4 + (w % 4 + dy) % 4
-    return w2, (l // 2 + dx) % 4 * 2 + (l % 2 + dc) % 2
+def wave_at(w, index):
+    dz = select8(index % 8, Z_ORDER)
+    dy = select8(index // 8, Y_ORDER)
+    return (w // 4 + dz) % 8 * 4 + (w % 4 + dy) % 4
 
 
 def sub_iota(shape):
@@ -263,7 +259,8 @@
 
     def send_forward(i, c):
         j = 256 - i
-        w2, l2 = target(w, l, j // 128, j % 128)
+        w2 = wave_at(w, j % NWAVE)
+        l2 = lev_at(l, j // NWAVE)
         d = w2 * NLEV + l2
         send_f[d] = packed(d)
         pltpu.make_async_remote_copy(
@@ -415,15 +412,9 @@
             ]
             for u, x in enumerate(swap_lane(*tiles)):
                 send_b[(4 * block + u) * NLEV + l2] = x.astype(BF16)
-        return c
-
-    for half in range(2):
-        lax.fori_loop(4 * half, 4 * half + 4, arrive, 0)
-        legendre_step(half)
-        lax.fori_loop(4 * half, 4 * half + 4, send_group, 0)
-
-        def send_back(m, c, half=half):
-            w2, l2 = target(w, l, 1 - half, 127 - m)
+
+        def send_back(m, c):
+            w2 = wave_at(w, 31 - m)
             d = w2 * NLEV + l2
 
             @pl.when(d != me)
@@ -435,7 +426,13 @@
 
             return c
 
-        lax.fori_loop(0, 128, send_back, 0)
+        lax.fori_loop(0, 32, send_back, 0)
+        return c
+
+    for half in range(2):
+        lax.fori_loop(4 * half, 4 * half + 4, arrive, 0)
+        legendre_step(half)
+        lax.fori_loop(4 * half, 4 * half + 4, send_group, 0)
     recv_b[me] = send_b[me]
 
     holders = [jnp.zeros((1, 128), F32)] * 4

time: 83.5 us -> 78.6 us (0.941)
  Pallas kernels: 80.6 us -> 75.8 us
    pallas_call x1, Pallas kernels: 80.6 us -> 75.8 us  [shards(): pl.pallas_call(exchange, out_shape=(pltpu.VMEM((2, 32, 2, ROWS), F32), pl...]
where the time goes in v5:
time: 78.6 us
  Pallas kernels  75.8 us (96%)
  local copies, waits for them, and re-layouts  2.16 us (3%)
    pallas_call x1, Pallas kernels, shards(): pl.pallas_call(exchange, out_shape=(pltpu.VMEM((2, 32, 2, ROWS), F32), pl...  75.8 us
    unnamed x2, local copies, waits for them, and re-layouts  2.16 us

profile of v5, /device:TPU:2, one launch (start us, length us, event | category | flops | bytes accessed | tf_op | source)
XLA Modules:
  0.0 78.6 jit_solution(10805572794580435396)
XLA Ops:
  0.6 75.8 %exchange.1 = (f32[2,32,2,1025]{3,2,1,0:T(2,128)S(1)}, bf16[4,2,32,4224]{3,2,1,0:T(8,128)(2,1)S(1)}) custom-call(bf16[4,2,32,4224]{3,2,1,0:T(8,128)(2,1)} %field_hbm.1, bf16[1025,8,2,128]{3,2,1,0:T(2,128)(2,1)} %bitcast.4, bf16[2,1024,2176]{2,1,0:T(8,128)(2,1)} %constant.2.clone.table_hbm, s32[2]{0:T(128)} %ids_hbm.1, f32[1,1024]{1,0:T(1,128)} %bitcast.5, ...), custom_call_target="tpu_custom_call" | custom-call | tf_op jit(solution)/shard_map/exchange/pallas_call | solution.py:546
  76.4 0.8 %copy.11 = f32[2,32,2,1025]{3,2,1,0:T(2,128)} copy(f32[2,32,2,1025]{3,2,1,0:T(2,128)S(1)} %get-tuple-element.2) | data formatting | bytes 1049600
  77.2 1.3 %copy.12 = bf16[4,2,32,4224]{3,2,1,0:T(8,128)(2,1)} copy(bf16[4,2,32,4224]{3,2,1,0:T(8,128)(2,1)S(1)} %get-tuple-element.3) | data formatting | bytes 4325376

commit v6 on v5

--- a/solution.py
+++ b/solution.py
@@ -281,7 +281,7 @@
                 leg[s, pl.ds(k, 16), ch * 128:(ch + 1) * 128] = x[:, s, :].astype(BF16)
         return c
 
-    lax.fori_loop(0, 64, relay, 0)
+    lax.fori_loop(0, 64, relay, 0, unroll=2)
     for ch in range(8):
         x = raw[1024, ch].astype(F32)
         for s in range(2):
@@ -426,7 +426,7 @@
 
             return c
 
-        lax.fori_loop(0, 32, send_back, 0)
+        lax.fori_loop(0, 32, send_back, 0, unroll=4)
         return c
 
     for half in range(2):

time: 78.6 us -> 78.5 us (level)
  no operation moved by 1% of the time
where the time goes in v6:
time: 78.5 us; the launch traced here: 78.4 us
  Pallas kernels  75.6 us (96%)
  local copies, waits for them, and re-layouts  2.16 us (3%)
    pallas_call x1, Pallas kernels, shards(): pl.pallas_call(exchange, out_shape=(pltpu.VMEM((2, 32, 2, ROWS), F32), pl...  75.6 us
    unnamed x2, local copies, waits for them, and re-layouts  2.16 us

profile of v6, /device:TPU:2, one launch (start us, length us, event | category | flops | bytes accessed | tf_op | source)
XLA Modules:
  0.0 78.4 jit_solution(5193460906613817647)
XLA Ops:
  0.6 75.6 %exchange.1 = (f32[2,32,2,1025]{3,2,1,0:T(2,128)S(1)}, bf16[4,2,32,4224]{3,2,1,0:T(8,128)(2,1)S(1)}) custom-call(bf16[4,2,32,4224]{3,2,1,0:T(8,128)(2,1)} %field_hbm.1, bf16[1025,8,2,128]{3,2,1,0:T(2,128)(2,1)} %bitcast.4, bf16[2,1024,2176]{2,1,0:T(8,128)(2,1)} %constant.2.clone.table_hbm, s32[2]{0:T(128)} %ids_hbm.1, f32[1,1024]{1,0:T(1,128)} %bitcast.5, ...), custom_call_target="tpu_custom_call" | custom-call | tf_op jit(solution)/shard_map/exchange/pallas_call | solution.py:546
  76.2 0.8 %copy.11 = f32[2,32,2,1025]{3,2,1,0:T(2,128)} copy(f32[2,32,2,1025]{3,2,1,0:T(2,128)S(1)} %get-tuple-element.2) | data formatting | bytes 1049600
  77.0 1.3 %copy.12 = bf16[4,2,32,4224]{3,2,1,0:T(8,128)(2,1)} copy(bf16[4,2,32,4224]{3,2,1,0:T(8,128)(2,1)S(1)} %get-tuple-element.3) | data formatting | bytes 4325376
